TPU v7x, 32 devices: a whole 2x2x4 slice. The times are simulated.
32 devices in a mesh: ens: 2 (over x), lon: 16 (over z, y, core).
Axes of the slice: x: 2, y: 2, z: 4, core: 2. Of those that a mesh axis runs over, the one named last changes fastest.
Arguments:
- state_in: bfloat16 [32, 128, 512], P('ens', 'lon'), parts along dimension 0, may hold values from -6 to 6
- ocean_mask: int32 [16, 128], P(None, 'lon'), may hold values 0 or 1
- fold_partner: int32 [128], replicated, may hold values from 0 to 127, as said below
- depth_kernel: float32 [49, 512], replicated, may hold values from -0.875 to 0.875
- norm_gain: float32 [512], replicated, may hold values from 0.1 to 1.9
- norm_bias: float32 [512], replicated, may hold values from -3 to 3
- w_up: bfloat16 [512, 2048], replicated, may hold values from -0.25 to 0.25
- w_down: bfloat16 [2048, 512], replicated, may hold values from -0.125 to 0.125
- cotangent: bfloat16 [32, 128, 512], P('ens', 'lon'), parts along dimension 0, may hold values from -8 to 8
Outputs:
- out_state: bfloat16 [32, 128, 512], P('ens', 'lon'), parts along dimension 0
- grad_state: bfloat16 [32, 128, 512], P('ens', 'lon'), parts along dimension 0
- grad_up: float32 [1024, 2048], P(('ens', 'lon')), parts along dimension 0
- grad_down: float32 [4096, 512], P(('ens', 'lon')), parts along dimension 0
- grad_kernel: float32 [98, 512], P('ens'), parts along dimension 0
- grad_gain: float32 [1024], P('ens'), parts along dimension 0
- grad_bias: float32 [1024], P('ens'), parts along dimension 0
There are 2 independent parts, one for each index of `ens`. A program takes and returns all parts, laid end to end along the dimension named above; an argument that names none is the same for every part. Nothing has to cross between parts.
Inputs may be any that keep to these rules, and one draw needn't show every extreme that they name: fold_partner[i] == (P - i) mod 128 for every column i, with one whole number P of 0 to 127 in each draw.
All inputs are finite; a program needn't handle non-finite values. No bound on the sum of `ocean_mask` on one device may be relied on, other than what follows from the above.
Results may differ from a plain program's by a relative error of at most 0.0055.
Values may be sent and summed in bfloat16 or wider, within the bound.
A program may use at most 64 MiB of HBM per device.

v0:
```python
import math

import jax
import jax.numpy as jnp
from jax import lax
from jax.sharding import PartitionSpec as P

EPS = 1e-06


def with_halo(cells, sides, width):
    for axis, dim in sides:
        count = lax.axis_size(axis)
        head = lax.slice_in_dim(cells, 0, width, axis=dim)
        tail = lax.slice_in_dim(cells, cells.shape[dim] - width, cells.shape[dim], axis=dim)
        cells = jnp.concatenate(
            [
                lax.ppermute(tail, axis, [(i, (i + 1) % count) for i in range(count)]),
                cells,
                lax.ppermute(head, axis, [((i + 1) % count, i) for i in range(count)]),
            ],
            axis=dim,
        )
    return cells


def gelu_value(values):
    return jax.nn.gelu(values, approximate=True)


def gelu_back(values, upstream):
    return jax.vjp(gelu_value, values)[1](upstream)[0]


def depth_conv(extended, depth_kernel):
    channels = extended.shape[2]
    result = lax.conv_general_dilated(
        extended[None],
        depth_kernel.reshape(7, 7, 1, channels),
        (1, 1),
        "VALID",
        dimension_numbers=("NHWC", "HWIO", "NHWC"),
        feature_group_count=channels,
        precision=lax.Precision.HIGHEST,
    )
    return result[0]


def on_device(
    state_in, ocean_mask, fold_partner, depth_kernel, norm_gain, norm_bias, w_up, w_down, cotangent
):
    lat_rows, lon_cols, channels = state_in.shape
    hidden_units = w_up.shape[1]
    devices = lax.axis_size("lon")
    total_lon = lon_cols * devices
    grad_scale = 1.0 / math.sqrt(lat_rows * total_lon)
    mask_bf = ocean_mask[:, :, None].astype(jnp.bfloat16)
    mask_float = ocean_mask[:, :, None].astype(jnp.float32)
    masked = state_in * mask_bf
    zonal_ext = with_halo(masked, (("lon", 1),), 3)
    whole_top = lax.all_gather(masked[lat_rows - 3 :], "lon", axis=1, tiled=True)
    first_col = lax.axis_index("lon") * lon_cols
    own_cols = first_col + jnp.arange(lon_cols)
    ext_cols = (first_col - 3 + jnp.arange(lon_cols + 6)) % total_lon
    north_rows = jnp.take(whole_top, jnp.take(fold_partner, ext_cols), axis=1)[::-1]
    south_pad = jnp.zeros((3, lon_cols + 6, channels), jnp.bfloat16)
    extended = jnp.concatenate([south_pad, zonal_ext, north_rows], axis=0).astype(jnp.float32)
    conv_out, conv_back = jax.vjp(depth_conv, extended, depth_kernel)
    row_count = lat_rows * lon_cols
    conv_rows = conv_out.reshape(row_count, channels)
    centred = conv_rows - jnp.mean(conv_rows, axis=1, keepdims=True)
    inv_std = 1.0 / jnp.sqrt(jnp.mean(centred * centred, axis=1, keepdims=True) + EPS)
    normed = centred * inv_std
    norm_out = (normed * norm_gain + norm_bias).astype(jnp.bfloat16)
    pre_act = jnp.dot(norm_out, w_up, preferred_element_type=jnp.float32)
    hidden_u = gelu_value(pre_act).astype(jnp.bfloat16)
    branch = jnp.dot(hidden_u, w_down, preferred_element_type=jnp.float32)
    out_state = (
        state_in.astype(jnp.float32) + mask_float * branch.reshape(lat_rows, lon_cols, channels)
    ).astype(jnp.bfloat16)
    upstream = (cotangent * mask_bf).reshape(row_count, channels)
    grad_hidden = lax.dot_general(
        upstream, w_down, (((1,), (1,)), ((), ())), preferred_element_type=jnp.float32
    )
    grad_pre = gelu_back(pre_act, grad_hidden).astype(jnp.bfloat16)
    part_norm = lax.slice_in_dim(norm_out, 0, channels // devices * lax.axis_size("lon"), axis=1)
    grad_up = (
        lax.psum_scatter(
            lax.dot_general(
                part_norm, grad_pre, (((0,), (0,)), ((), ())), preferred_element_type=jnp.float32
            ),
            "lon",
            scatter_dimension=0,
            tiled=True,
        )
        * grad_scale
    )
    grad_norm = lax.dot_general(
        grad_pre, w_up, (((1,), (1,)), ((), ())), preferred_element_type=jnp.float32
    )
    gain_part = jnp.sum(grad_norm * normed, axis=0)
    bias_part = jnp.sum(grad_norm, axis=0)
    gain_sum, bias_sum = lax.psum((gain_part, bias_part), "lon")
    scaled = grad_norm * norm_gain
    grad_conv = (
        scaled
        - jnp.mean(scaled, axis=1, keepdims=True)
        - normed * jnp.mean(scaled * normed, axis=1, keepdims=True)
    ) * inv_std
    grad_ext, kernel_part = conv_back(grad_conv.reshape(lat_rows, lon_cols, channels))
    kernel_sum = lax.psum(kernel_part, "lon")
    middle = grad_ext[3:]
    margins = jnp.concatenate([middle[:, :3], middle[:, lon_cols + 3 :]], axis=1)
    returned = with_halo(margins.astype(jnp.bfloat16), (("lon", 1),), 3).astype(margins.dtype)
    inner_grad = middle[:, 3 : lon_cols + 3]
    inner_grad = inner_grad.at[:, :3].add(returned[:, :3])
    inner_grad = inner_grad.at[:, lon_cols - 3 :].add(returned[:, 9:])
    north_grad = inner_grad[lat_rows:]
    partner_own = jnp.take(fold_partner, own_cols)
    whole_north = lax.all_gather(north_grad.astype(jnp.bfloat16), "lon", axis=1, tiled=True).astype(
        north_grad.dtype
    )
    own_fold = jnp.take(whole_north, partner_own, axis=1)
    grad_masked = inner_grad[:lat_rows].at[lat_rows - 3 :].add(own_fold[::-1])
    grad_state = (cotangent.astype(jnp.float32) + mask_float * grad_masked).astype(jnp.bfloat16)
    part_hidden = lax.slice_in_dim(
        hidden_u, 0, hidden_units // devices * lax.axis_size("lon"), axis=1
    )
    grad_down = (
        lax.psum_scatter(
            lax.dot_general(
                part_hidden, upstream, (((0,), (0,)), ((), ())), preferred_element_type=jnp.float32
            ),
            "lon",
            scatter_dimension=0,
            tiled=True,
        )
        * grad_scale
    )
    return (
        out_state,
        grad_state,
        grad_up,
        grad_down,
        kernel_sum * grad_scale,
        gain_sum * grad_scale,
        bias_sum * grad_scale,
    )


def solution(mesh):
    return jax.shard_map(
        on_device,
        mesh=mesh,
        in_specs=(
            P("ens", "lon", None),
            P(None, "lon"),
            P(),
            P(),
            P(),
            P(),
            P(),
            P(),
            P("ens", "lon", None),
        ),
        out_specs=(
            P("ens", "lon", None),
            P("ens", "lon", None),
            P(("ens", "lon"), None),
            P(("ens", "lon"), None),
            P("ens", None),
            P("ens"),
            P("ens"),
        ),
        check_vma=False,
    )
```

profile of v0, /device:TPU:0, one launch (start us, length us, event | category | flops | bytes accessed | tf_op | source)
XLA Modules:
  0.0 306.4 jit_solution(6807996089846510440)
XLA Ops:
  7.2 0.0 all-reduce.3.cloned.1.call-start
  7.2 0.9 fusion.40
  8.1 1.1 copy_multiply_fusion
  9.2 0.5 collective-permute-start
  9.7 5.1 %collective-permute-start.1 = (bf16[16,3,512]{2,0,1:T(8,128)(2,1)S(1)}, bf16[16,3,512]{2,0,1:T(8,128)(2,1)S(1)}, u32[]{:S(2)}, u32[]{:S(2)}) collective-permute-start(bf16[16,3,512]{2,0,1:T(8,128)(2,1)S(1)} %get-tuple-element.52), channel_id=1, source_target_pairs={{1,0},{2,1},{3,2},{4,3},{5,4},{6,5},{7,6},{8,7},{9,8},{10,9},{11,1... | collective-permute-start | bytes 147464 | tf_op jit(solution)/shard_map/ppermute | solution.py:20
  14.8 1.3 gather_fusion
  16.2 20.4 %all_gather.6 = bf16[3,128,512]{2,1,0:T(8,128)(2,1)S(1)} all-gather(bf16[3,8,512]{2,1,0:T(8,128)(2,1)S(1)} %copy.47), channel_id=1, replica_groups=mesh['ens'=2,'lon'=16] {'lon'}, dimensions={1}, use_global_device_ids=true | all-gather | bytes 417792 | tf_op jit(solution)/shard_map/all_gather | solution.py:61
  36.6 0.3 copy.48
  36.9 0.6 gather_fusion.1
  37.5 0.1 select_bitcast_fusion
  37.7 0.1 reshape.344
  37.8 0.2 rev.7
  38.1 0.2 maximum_bitcast_fusion
  38.3 2.9 fusion.41
  41.2 0.1 div.17
  41.3 0.6 multiply_reduce_fusion.2
  41.9 0.1 sqrt.6
  42.0 1.3 fusion.28
  43.3 0.3 copy-done.15
  43.6 1.1 fusion.9
  44.7 0.8 copy-done.2
  45.5 1.5 multiply_reduce_fusion
  47.0 0.1 multiply_bitcast_fusion
  47.2 0.7 copy-done.8
  47.9 11.2 %convolution_reduce_fusion = f32[7,7,512]{2,1,0:T(8,128)} fusion(bf16[1,22,14,512]{3,1,2,0:T(8,128)(2,1)S(1)} %copy-done.7, f32[1,16,8,512]{3,2,1,0:T(8,128)S(1)} %multiply_bitcast_fusion), kind=kOutput, calls=%fused_computation.10 | convolution fusion | flops 38535168 | bytes 677888 | tf_op jit(solution)/shard_map/transpose(jvp())/conv_general_dilated | solution.py:37
  59.1 1.6 reshape.311
  60.6 0.0 all-reduce.3.cloned.1.call-update
  60.6 0.0 reduce-scatter.5.cloned.1.call-start
  60.7 2.8 fusion.17
  63.5 0.0 reduce-scatter.5.cloned.1.call-update
  63.5 0.0 reduce-scatter.3.cloned.1.call-start
  63.5 0.6 copy-done.11
  64.2 3.8 %fusion.27 = f32[512,2048]{1,0:T(8,128)} fusion(bf16[128,2048]{1,0:T(8,128)(2,1)} %copy-done.2, f32[512]{0:T(512)S(1)} %copy-done.11, f32[512]{0:T(512)S(1)} %copy-done.10, f32[1,16,8,512]{3,0,2,1:T(1,128)S(1)} %get-tuple-element.58, f32[128]{0:T(128)S(1)} %sqrt.6, f32[128]{0:T(128)S(1)} %div.17), kind=kOutput, calls=%fused_computation.58 | convolution fusion | flops 268763136 | bytes 4985856 | tf_op jit(solution)/shard_map/dot_general | solution.py:89
  68.0 0.0 reduce-scatter.3.cloned.1.call-update
  68.0 0.9 copy-done.5
  68.8 0.8 reshape.345
  69.6 0.6 gather_fusion.2
  70.3 0.1 copy.45
  70.4 0.5 compare_and_fusion
  70.9 3.8 %fusion.15 = f32[1,19,14,512]{3,0,2,1:T(1,128)S(1)} fusion(f32[7,7,512,1]{2,3,1,0:T(1,128)} %reshape.345, f32[1,16,8,512]{3,2,1,0:T(8,128)S(1)} %copy-done.9), kind=kOutput, calls=%fused_computation.36 | convolution fusion | flops 36470784 | bytes 907264 | tf_op jit(solution)/shard_map/slice | solution.py:112
  74.8 0.1 copy.101
  74.9 0.8 fusion.38
  75.7 0.3 collective-permute-start.2
  76.1 4.1 %collective-permute-start.3 = (bf16[19,3,512]{2,1,0:T(4,128)(2,1)}, bf16[19,3,512]{2,1,0:T(4,128)(2,1)}, u32[]{:S(2)}, u32[]{:S(2)}) collective-permute-start(bf16[19,3,512]{2,1,0:T(4,128)(2,1)} %get-tuple-element.50), channel_id=1, source_target_pairs={{1,0},{2,1},{3,2},{4,3},{5,4},{6,5},{7,6},{8,7},{9,8},{10,9},{11,1... | collective-permute-start | bytes 175112 | tf_op jit(solution)/shard_map/ppermute | solution.py:20
  80.2 30.1 %all-reduce = (f32[512]{0:T(512)}, f32[512]{0:T(512)}) all-reduce(f32[512]{0:T(512)S(1)} %copy-done.12, f32[512]{0:T(512)S(1)} %copy-done.13), channel_id=1, replica_groups=mesh['ens'=2,'lon'=16] {'lon'}, use_global_device_ids=true, to_apply=%region_8.9 | all-reduce | flops 1024 | bytes 8192 | tf_op jit(solution)/shard_map/psum | solution.py:103
  110.4 1.3 broadcast_multiply_fusion.4
  111.6 2.8 fusion.2
  114.5 29.4 %all-reduce.3.cloned.1.call-done = f32[49,512]{1,0:T(8,128)} async-done(((f32[49,512]{1,0:T(8,128)}), f32[49,512]{1,0:T(8,128)}) %all-reduce.3.cloned.1.call-update) | async-done | bytes 100368 | tf_op jit(solution)/shard_map/psum | solution.py:111
  143.9 1.6 broadcast_multiply_fusion.2
  145.4 1.2 convert_add_fusion
  146.7 1.1 scatter-add.10
  147.8 1.1 slice_add_fusion
  148.9 1.1 scatter-add.11
  150.0 0.7 slice.146
  150.7 23.7 %all_gather.7 = bf16[3,128,512]{2,1,0:T(8,128)(2,1)S(1)} all-gather(bf16[3,8,512]{2,1,0:T(8,128)(2,1)S(1)} %slice.156), channel_id=1, replica_groups=mesh['ens'=2,'lon'=16] {'lon'}, dimensions={1}, use_global_device_ids=true | all-gather | bytes 417792 | tf_op jit(solution)/shard_map/all_gather | solution.py:120
  174.4 0.3 copy.55
  174.7 0.6 gather_fusion.3
  175.3 0.1 fusion.26
  175.4 0.6 fusion.25
  176.0 1.7 add_convert_fusion
  177.8 44.7 %reduce-scatter.5.cloned.1.call-done = f32[128,512]{1,0:T(8,128)} async-done(((f32[2048,512]{1,0:T(8,128)}), f32[128,512]{1,0:T(8,128)}) %reduce-scatter.5.cloned.1.call-update) | async-done | bytes 262160 | tf_op jit(solution)/shard_map/reduce_scatter | solution.py:130
  222.5 1.7 broadcast_multiply_fusion
  224.1 74.1 %reduce-scatter.3.cloned.1.call-done = f32[32,2048]{1,0:T(8,128)} async-done(((f32[512,2048]{1,0:T(8,128)}), f32[32,2048]{1,0:T(8,128)}) %reduce-scatter.3.cloned.1.call-update) | async-done | bytes 262160 | tf_op jit(solution)/shard_map/reduce_scatter | solution.py:88
  298.2 1.7 broadcast_multiply_fusion.1
  (51 shorter events, 0.3 us)
Async XLA Ops:
  7.2 34.8 %copy-start = (bf16[512,2048]{1,0:T(8,128)(2,1)S(1)}, bf16[512,2048]{1,0:T(8,128)(2,1)}, u32[]{:S(2)}) copy-start(bf16[512,2048]{1,0:T(8,128)(2,1)} %param.21) | copy-start | bytes 6291460
  7.2 30.5 %copy-start.4 = (f32[49,512]{1,0:T(8,128)S(1)}, f32[49,512]{1,0:T(8,128)}, u32[]{:S(2)}) copy-start(f32[49,512]{1,0:T(8,128)} %param.18) | copy-start | bytes 301060
  7.2 136.7 %all-reduce.3.cloned.1.call-start = ((), (), s32[]{:S(2)}) async-start(), calls=%async_computation.4 | async-start | bytes 229376 | tf_op jit(solution)/shard_map/psum | solution.py:111
  9.2 28.9 %collective-permute-start = (bf16[16,3,512]{2,0,1:T(8,128)(2,1)S(1)}, bf16[16,3,512]{2,0,1:T(8,128)(2,1)S(1)}, u32[]{:S(2)}, u32[]{:S(2)}) collective-permute-start(bf16[16,3,512]{2,0,1:T(8,128)(2,1)S(1)} %get-tuple-element.51), channel_id=1, source_target_pairs={{0,1},{1,2},{2,3},{3,4},{4,5},{5,6},{6,7},{7,8},{8,9},{9,10},{10,1... | collective-permute-start | bytes 147464 | tf_op jit(solution)/shard_map/ppermute | solution.py:18
  9.7 28.4 %collective-permute-start.1 = (bf16[16,3,512]{2,0,1:T(8,128)(2,1)S(1)}, bf16[16,3,512]{2,0,1:T(8,128)(2,1)S(1)}, u32[]{:S(2)}, u32[]{:S(2)}) collective-permute-start(bf16[16,3,512]{2,0,1:T(8,128)(2,1)S(1)} %get-tuple-element.52), channel_id=1, source_target_pairs={{1,0},{2,1},{3,2},{4,3},{5,4},{6,5},{7,6},{8,7},{9,8},{10,9},{11,1... | collective-permute-start | bytes 147464 | tf_op jit(solution)/shard_map/ppermute | solution.py:20
  38.2 2.9 copy-start.6
  38.3 3.7 %copy-start.10 = (f32[512]{0:T(512)S(1)}, f32[512]{0:T(512)}, u32[]{:S(2)}) copy-start(f32[512]{0:T(512)} %param.19) | copy-start | bytes 6148
  42.0 1.6 copy-start.15
  44.7 0.8 copy-start.2
  45.5 2.3 copy-start.7
  47.2 0.7 copy-start.8
  60.6 161.8 %reduce-scatter.5.cloned.1.call-start = ((), (), s32[]{:S(2)}) async-start(), calls=%async_computation.3 | async-start | bytes 4456448 | tf_op jit(solution)/shard_map/reduce_scatter | solution.py:130
  63.5 0.7 copy-start.11
  63.5 234.7 %reduce-scatter.3.cloned.1.call-start = ((), (), s32[]{:S(2)}) async-start(), calls=%async_computation.2 | async-start | bytes 4456448 | tf_op jit(solution)/shard_map/reduce_scatter | solution.py:88
  67.9 0.9 copy-start.5
  67.9 1.7 copy-start.1
  67.9 2.9 copy-start.9
  74.7 5.5 %copy-start.12 = (f32[512]{0:T(512)S(1)}, f32[512]{0:T(512)}, u32[]{:S(2)}) copy-start(f32[512]{0:T(512)} %get-tuple-element.43) | copy-start | bytes 6148
  74.8 5.5 %copy-start.13 = (f32[512]{0:T(512)S(1)}, f32[512]{0:T(512)}, u32[]{:S(2)}) copy-start(f32[512]{0:T(512)} %get-tuple-element.46) | copy-start | bytes 6148
  74.9 5.3 %copy-start.3 = (f32[1,19,14,512]{3,2,0,1:T(8,128)}, f32[1,19,14,512]{3,2,0,1:T(8,128)S(1)}, u32[]{:S(2)}) copy-start(f32[1,19,14,512]{3,2,0,1:T(8,128)S(1)} %copy.101) | copy-start | bytes 1634308
  75.7 69.7 %collective-permute-start.2 = (bf16[19,3,512]{2,1,0:T(4,128)(2,1)S(1)}, bf16[19,3,512]{2,1,0:T(4,128)(2,1)}, u32[]{:S(2)}, u32[]{:S(2)}) collective-permute-start(bf16[19,3,512]{2,1,0:T(4,128)(2,1)S(1)} %get-tuple-element.49), channel_id=1, source_target_pairs={{0,1},{1,2},{2,3},{3,4},{4,5},{5,6},{6,7},{7,8},{8,9},{9,10},{10,1... | collective-permute-start | bytes 175112 | tf_op jit(solution)/shard_map/ppermute | solution.py:18
  76.1 69.4 %collective-permute-start.3 = (bf16[19,3,512]{2,1,0:T(4,128)(2,1)}, bf16[19,3,512]{2,1,0:T(4,128)(2,1)}, u32[]{:S(2)}, u32[]{:S(2)}) collective-permute-start(bf16[19,3,512]{2,1,0:T(4,128)(2,1)} %get-tuple-element.50), channel_id=1, source_target_pairs={{1,0},{2,1},{3,2},{4,3},{5,4},{6,5},{7,6},{8,7},{9,8},{10,9},{11,1... | collective-permute-start | bytes 175112 | tf_op jit(solution)/shard_map/ppermute | solution.py:20
  145.4 29.9 %copy-start.14 = (pred[8]{0:T(512)(128)(4,1)S(1)}, pred[8]{0:T(512)(128)(4,1)}, u32[]{:S(2)}) copy-start(pred[8]{0:T(512)(128)(4,1)} %compare_and_fusion) | copy-start | bytes 28
Sparse Core Ops, SparseCore 0:
  60.8 83.0 all-reduce.2
  147.7 74.6 reduce-scatter.4
  226.8 71.3 reduce-scatter.2
where the time goes:
time: 307 us; the launch traced here: 306 us
  waiting for transfers between devices  148 us (48%)
  blocking collectives  74.2 us (24%)
  matrix products  31.2 us (10%)
  other arithmetic  14.5 us (5%)
  local copies, waits for them, and re-layouts  14.1 us (5%)
  between operations  14.1 us (5%)
  starting transfers between devices  10.1 us (3%)
    reduce_scatter x1, waiting for transfers between devices, on_device(): lax.psum_scatter(lax.dot_general(part_norm, grad_pre, (((0,), (0,)), ((),...  74.1 us
    reduce_scatter x1, waiting for transfers between devices, on_device(): lax.psum_scatter(lax.dot_general(part_hidden, upstream, (((0,), (0,)), ((...  44.7 us
    psum x1, blocking collectives, on_device(): gain_sum, bias_sum = lax.psum((gain_part, bias_part), 'lon')  30.1 us
    psum x1, waiting for transfers between devices, on_device(): kernel_sum = lax.psum(kernel_part, 'lon')  29.4 us
    all_gather x1, blocking collectives, on_device(): lax.all_gather(north_grad.astype(jnp.bfloat16), 'lon', axis=1, tiled=True)  23.7 us
    all_gather x1, blocking collectives, on_device(): whole_top = lax.all_gather(masked[lat_rows - 3:], 'lon', axis=1, tiled=True)  20.4 us
    conv_general_dilated x2, matrix products, depth_conv(): lax.conv_general_dilated(extended[None], depth_kernel.reshape(7, 7, 1, ch...  14.1 us
    ppermute x2, starting transfers between devices, with_halo(): lax.ppermute(head, axis, [((i + 1) % count, i) for i in range(count)])  9.15 us
  transfers between devices with their start and end apart: 7, of which 3 were waited for; matrix products, arithmetic and copies ran while one was open for 11% of the time, Pallas kernels for 0%

commit v1 on v0

v1 whole, which is shorter than its diff:
```python
import functools
import math

import jax
import jax.numpy as jnp
import numpy as np
from jax import lax
from jax.experimental import pallas as pl
from jax.experimental.pallas import tpu as pltpu
from jax.sharding import PartitionSpec as P

EPS = 1e-06
TILE = 512
BF = jnp.bfloat16
F32 = jnp.float32
GELU_A = math.sqrt(2.0 / math.pi)
GELU_B = 0.044715


def shift_matrices(lat, cols):
    own0, right0 = 3 * lat, 3 * lat + lat * cols
    depth = -(-(right0 + 3 * lat) // 128) * 128
    shifts = np.zeros((7, lat, cols, depth), np.float32)
    for b in range(7):
        for i in range(cols):
            e = b + i
            for r in range(lat):
                if e < 3:
                    src = r * 3 + e
                elif e < cols + 3:
                    src = own0 + r * cols + e - 3
                else:
                    src = right0 + r * 3 + e - cols - 3
                shifts[b, r, i, src] = 1.0
    packs = np.zeros((2, lat, 3, lat * cols), np.float32)
    for r in range(lat):
        for k in range(3):
            packs[0, r, k, r * cols + k] = 1.0
            packs[1, r, k, r * cols + cols - 3 + k] = 1.0
    return shifts.reshape(7 * lat * cols, depth), packs.reshape(6 * lat, lat * cols)


def place(chunk, order):
    pos = 0
    for bit in order:
        pos = pos * 2 + (chunk // 2**bit) % 2
    return pos


def dot(a, b, dims=((1,), (0,))):
    return lax.dot_general(a, b, (dims, ((), ())), preferred_element_type=F32)


def kernel(
    n, lat, cols,
    fold_ref, state_ref, mask_ref, dk_ref, gain_ref, bias_ref, cot_ref, shift_ref, pack_ref, wup_hbm, wdn_hbm,
    out_ref, gstate_ref, gup_ref, gdn_ref, gk_ref, ggain_ref, gbias_ref,
    wup, wdn, ext, ext_g, pk, pk_g, top, top_g, sh, sh_g, sh_f, norm_s, nout_s, inv_s, ups, br, gn, gc,
    acc_d, acc_u, snd_d, snd_u, rcv_d, rcv_u, smb, smr,
    w_sem, h_send, h_recv, t_send, t_recv, d_send, d_recv, u_send, u_recv, s_send, s_recv,
):
    chans = state_ref.shape[1]
    hid = wup.shape[1]
    cells = lat * cols
    total = n * cols
    logn = n.bit_length() - 1
    scale = 1.0 / math.sqrt(lat * total)
    me = lax.axis_index("lon")
    order_d = list(range(logn))
    order_u = [0, 2, 1] + list(range(3, logn))
    right, left = (me + 1) % n, (me + n - 1) % n
    half_c = chans // 2

    w_copies = [
        pltpu.make_async_copy(wup_hbm, wup, w_sem.at[0]),
        pltpu.make_async_copy(wdn_hbm, wdn, w_sem.at[1]),
    ]
    for c in w_copies:
        c.start()

    barrier = pltpu.get_barrier_semaphore()

    @pl.loop(1, n)
    def _(k):
        pl.semaphore_signal(barrier, inc=1, device_id={"lon": (me + k) % n}, device_id_type=pl.DeviceIdType.MESH)

    mask = mask_ref[...]
    mask_bf = mask.astype(BF)

    def remote(src, dst, ss, rs, dev):
        return pltpu.make_async_remote_copy(
            src_ref=src, dst_ref=dst, send_sem=ss, recv_sem=rs,
            device_id={"lon": dev}, device_id_type=pl.DeviceIdType.MESH,
        )

    own0, right0, edge = 3 * lat, 3 * lat + cells, 3 * lat

    def halo_copies(e_ref, p_ref, w):
        return [
            remote(p_ref.at[pl.ds(edge, edge)], e_ref.at[pl.ds(0, edge)], h_send.at[2 * w], h_recv.at[2 * w], right),
            remote(p_ref.at[pl.ds(0, edge)], e_ref.at[pl.ds(right0, edge)], h_send.at[2 * w + 1], h_recv.at[2 * w + 1], left),
        ]

    def top_copy(t_ref, w, k):
        return remote(t_ref.at[me], t_ref.at[me], t_send.at[w * n + k], t_recv.at[w * n + k], (me + k) % n)

    def prepare(e_ref, p_ref, t_ref, values_bf):
        e_ref[pl.ds(own0, cells), :] = values_bf
        e_ref[pl.ds(right0 + edge, e_ref.shape[0] - right0 - edge), :] = jnp.zeros(
            (e_ref.shape[0] - right0 - edge, chans), BF)
        p_ref[...] = dot(pack_ref[...], values_bf).astype(BF)
        for k in range(3):
            row = values_bf[(lat - 3 + k) * cols:(lat - 2 + k) * cols].astype(F32)
            t_ref[me, pl.ds(k * 2 * cols, 2 * cols), :] = jnp.concatenate(
                [row[:, :half_c], row[:, half_c:]], axis=0).astype(BF)

    def send_all(e_ref, p_ref, t_ref, w):
        for c in halo_copies(e_ref, p_ref, w):
            c.start()

        @pl.loop(1, n)
        def _(k):
            top_copy(t_ref, w, k).start()

    def wait_halo(e_ref, p_ref, w):
        for c in halo_copies(e_ref, p_ref, w):
            c.wait_recv()

    def wait_top(t_ref, w):
        @pl.loop(1, n)
        def _(k):
            top_copy(t_ref, w, k).wait_recv()

    def put_shifts(e_ref, s_ref):
        s_ref[:, pl.ds(0, 3)] = jnp.zeros((7, 3, cols, chans), F32)
        for b in range(7):
            part = dot(shift_ref[pl.ds(b * cells, cells), :], e_ref[...])
            s_ref[b, pl.ds(3, lat)] = part.reshape(lat, cols, chans)

    def put_fold(t_ref, sel, store):
        for k in range(3):
            rows = t_ref[:, pl.ds(k * 2 * cols, 2 * cols), :].reshape(n * 2 * cols, half_c)
            got = dot(sel, rows).reshape(2, 7, cols, half_c)
            for h in range(2):
                for b in range(7):
                    store(k, b, pl.ds(h * half_c, half_c), got[h, b])

    def lanes(ct):
        return pl.ds(pl.multiple_of(ct * 128, 128), 128)

    state = state_ref[...]
    prepare(ext, pk, top, state * mask_bf)
    pl.semaphore_wait(barrier, n - 1)
    send_all(ext, pk, top, 0)

    m_id = lax.broadcasted_iota(jnp.int32, (14 * cols, n * 2 * cols), 0)
    q_id = lax.broadcasted_iota(jnp.int32, (14 * cols, n * 2 * cols), 1)
    half_m = jnp.where(m_id >= 7 * cols, 1, 0)
    m_in = m_id - half_m * (7 * cols)
    want = fold_ref[0] - me * cols + 3 - (m_in // cols + m_in % cols)
    want = jnp.where(want < 0, want + total, want)
    want = jnp.where(want < 0, want + total, want)
    want = jnp.where(want >= total, want - total, want)
    have = (q_id // (2 * cols)) * cols + q_id % cols
    half_q = (q_id // cols) % 2
    sel = jnp.where((have == want) & (half_q == half_m), 1.0, 0.0).astype(BF)

    cot = cot_ref[...]
    upstream = cot * mask_bf
    ups[...] = upstream

    wait_halo(ext, pk, 0)
    put_shifts(ext, sh)
    wait_top(top, 0)

    def store_north(k, b, ls, val):
        sh[b, lat + 5 - k, :, ls] = val

    put_fold(top, sel, store_north)

    @pl.loop(0, chans // 128)
    def _(ct):
        ls = lanes(ct)
        acc = jnp.zeros((lat, cols, 128), F32)
        for b in range(7):
            window = sh[b, :, :, ls]
            for a in range(7):
                tap = dk_ref[pl.ds(7 * a + b, 1), ls].reshape(1, 1, 128)
                acc = acc + tap * window[a:a + lat]
        norm_s[:, ls] = acc.reshape(cells, 128)

    conv = norm_s[...]
    centred = conv - jnp.mean(conv, axis=1, keepdims=True)
    inv = 1.0 / jnp.sqrt(jnp.mean(centred * centred, axis=1, keepdims=True) + EPS)
    inv_s[...] = inv
    normed = centred * inv
    norm_s[...] = normed
    nout_s[...] = (normed * gain_ref[...] + bias_ref[...]).astype(BF)
    for c in w_copies:
        c.wait()
    br[...] = jnp.zeros_like(br)
    gn[...] = jnp.zeros_like(gn)
    rows_d, rows_u = hid // n, chans // n
    per_tile = TILE // rows_d

    @pl.loop(0, hid // TILE)
    def _(t):
        hs = pl.ds(pl.multiple_of(t * TILE, TILE), TILE)
        nout = nout_s[...]
        up = ups[...]
        w1 = wup[:, hs]
        w2 = wdn[hs, :]
        v = dot(nout, w1)
        v2 = v * v
        th = jnp.tanh(GELU_A * (v + GELU_B * (v2 * v)))
        u = (0.5 * v * (1.0 + th)).astype(BF)
        br[...] += dot(u, w2)
        gd = dot(u, up, ((0,), (0,)))
        for cc in range(per_tile):
            pos = place(t * per_tile + cc, order_d)
            acc_d[pl.ds(pl.multiple_of(pos * rows_d, 8), rows_d), :] = gd[cc * rows_d:(cc + 1) * rows_d]
        gh = dot(up, w2, ((1,), (1,)))
        slope = 0.5 * (1.0 + th) + (0.5 * GELU_A) * v * (1.0 - th * th) * (1.0 + (3.0 * GELU_B) * v2)
        gp = (gh * slope).astype(BF)
        gn[...] += dot(gp, w1, ((1,), (1,)))
        gu = dot(nout, gp, ((0,), (0,)))
        for c in range(n):
            base = place(c, order_u) * (hid * chans // n // TILE)
            acc_u[pl.ds(pl.multiple_of(base + t * rows_u, 8), rows_u), :] = gu[c * rows_u:(c + 1) * rows_u]

    def bit_of(bit):
        return (me // 2**bit) % 2

    def partner(bit):
        return me + (1 - 2 * bit_of(bit)) * 2**bit

    size = acc_d.shape[0]

    def rs_base(order, s):
        base = 0
        for k in range(s):
            base = base + bit_of(order[k]) * (size >> (k + 1))
        return base

    def rs_copy(snd, rcv, ss, rs, order, s):
        off, half = size - (size >> s), size >> (s + 1)
        return remote(snd.at[pl.ds(off, half)], rcv.at[pl.ds(off, half)], ss.at[s], rs.at[s], partner(order[s]))

    def rs_send(acc, snd, rcv, ss, rs, order, s):
        off, half = size - (size >> s), size >> (s + 1)
        base = rs_base(order, s) + (1 - bit_of(order[s])) * half
        blk = min(64, half)

        @pl.loop(0, half // blk)
        def _(i):
            snd[pl.ds(pl.multiple_of(off + i * blk, 16), blk), :] = acc[
                pl.ds(pl.multiple_of(base + i * blk, 16), blk), :].astype(BF)

        rs_copy(snd, rcv, ss, rs, order, s).start()

    def rs_recv(acc, snd, rcv, ss, rs, order, s):
        off, half = size - (size >> s), size >> (s + 1)
        base = rs_base(order, s + 1)
        blk = min(64, half)
        rs_copy(snd, rcv, ss, rs, order, s).wait_recv()

        @pl.loop(0, half // blk)
        def _(i):
            at = pl.ds(pl.multiple_of(base + i * blk, 16), blk)
            acc[at, :] += rcv[pl.ds(pl.multiple_of(off + i * blk, 16), blk), :].astype(F32)

    down = (acc_d, snd_d, rcv_d, d_send, d_recv, order_d)
    upw = (acc_u, snd_u, rcv_u, u_send, u_recv, order_u)
    rs_send(*down, 0)
    rs_send(*upw, 0)

    gnorm = gn[...]
    normed = norm_s[...]
    gain_row = jnp.sum(gnorm * normed, axis=0, keepdims=True)
    bias_row = jnp.sum(gnorm, axis=0, keepdims=True)
    scaled = gnorm * gain_ref[...]
    grad_conv = (
        scaled
        - jnp.mean(scaled, axis=1, keepdims=True)
        - normed * jnp.mean(scaled * normed, axis=1, keepdims=True)
    ) * inv_s[...]
    gc[...] = grad_conv
    prepare(ext_g, pk_g, top_g, grad_conv.astype(BF))
    send_all(ext_g, pk_g, top_g, 1)
    taps = dk_ref.shape[0]
    smb[0, pl.ds(48, 8), :] = jnp.zeros((8, chans), F32)
    smb[0, pl.ds(taps, 1), :] = gain_row
    smb[0, pl.ds(taps + 1, 1), :] = bias_row

    out_ref[...] = (state_ref[...].astype(F32) + mask * br[...]).astype(BF)

    rs_recv(*down, 0)
    rs_send(*down, 1)
    rs_recv(*upw, 0)
    rs_send(*upw, 1)

    @pl.loop(0, chans // 128)
    def _(ct):
        ls = lanes(ct)
        g = gc[:, ls].reshape(lat, cols, 128)
        for b in range(7):
            window = sh[b, :, :, ls]
            for a in range(7):
                part = jnp.sum(g * window[a:a + lat], axis=0)
                smb[0, pl.ds(7 * a + b, 1), ls] = jnp.sum(part, axis=0, keepdims=True)

    def sm_copy(s):
        return remote(smb.at[s], smr.at[s], s_send.at[s], s_recv.at[s], partner(s))

    def sm_step(s):
        sm_copy(s).wait_recv()
        smb[s + 1] = smb[s] + smr[s]
        if s + 1 < logn:
            sm_copy(s + 1).start()

    sm_copy(0).start()

    wait_halo(ext_g, pk_g, 1)
    put_shifts(ext_g, sh_g)
    sh_g[:, pl.ds(lat + 3, 3)] = jnp.zeros((7, 3, cols, chans), F32)
    sm_step(0)
    wait_top(top_g, 1)

    def store_facing(k, b, ls, val):
        sh_f[b, k, :, ls] = val

    put_fold(top_g, sel, store_facing)

    @pl.loop(0, chans // 128)
    def _(ct):
        ls = lanes(ct)
        acc = jnp.zeros((lat, cols, 128), F32)
        fold = [jnp.zeros((cols, 128), F32) for _ in range(3)]
        for b in range(7):
            window = sh_g[b, :, :, ls]
            for a in range(7):
                tap = dk_ref[pl.ds(48 - (7 * a + b), 1), ls].reshape(1, 1, 128)
                acc = acc + tap * window[a:a + lat]
            for r in range(3):
                for j in range(3):
                    a = 8 - r - j
                    if a <= 6:
                        tap = dk_ref[pl.ds(7 * a + b, 1), ls]
                        fold[r] = fold[r] + tap * sh_f[b, j, :, ls]
        acc = acc.reshape(cells, 128)
        gc[:, ls] = acc
        for r in range(3):
            gc[pl.ds((lat - 3 + r) * cols, cols), ls] += fold[r]

    gstate_ref[...] = (cot_ref[...].astype(F32) + mask * gc[...]).astype(BF)

    for s in range(1, logn):
        rs_recv(*down, s)
        if s + 1 < logn:
            rs_send(*down, s + 1)
        rs_recv(*upw, s)
        if s + 1 < logn:
            rs_send(*upw, s + 1)
        sm_step(s)

    base_d = pl.multiple_of(rs_base(order_d, logn), 8)
    base_u = rs_base(order_u, logn)
    gdn_ref[...] = acc_d[pl.ds(base_d, rows_d), :] * scale
    for t in range(hid // TILE):
        gup_ref[:, pl.ds(t * TILE, TILE)] = acc_u[pl.ds(pl.multiple_of(base_u + t * rows_u, 8), rows_u), :] * scale
    gk_ref[...] = smb[logn, pl.ds(0, taps), :] * scale
    ggain_ref[...] = smb[logn, pl.ds(taps, 1), :] * scale
    gbias_ref[...] = smb[logn, pl.ds(taps + 1, 1), :] * scale

    for e_ref, p_ref, t_ref, w in ((ext, pk, top, 0), (ext_g, pk_g, top_g, 1)):
        for c in halo_copies(e_ref, p_ref, w):
            c.wait_send()

        @pl.loop(1, n)
        def _(k):
            top_copy(t_ref, w, k).wait_send()

    for s in range(logn):
        rs_copy(*down[1:], s).wait_send()
        rs_copy(*upw[1:], s).wait_send()
        sm_copy(s).wait_send()


def on_device(
    state_in, ocean_mask, fold_partner, depth_kernel, norm_gain, norm_bias, w_up, w_down, cotangent
):
    lat, cols, chans = state_in.shape
    hid = w_up.shape[1]
    n = lax.axis_size("lon")
    logn = n.bit_length() - 1
    cells = lat * cols
    shifts, packs = shift_matrices(lat, cols)
    depth = shifts.shape[1]
    rows = hid * chans // TILE
    vm = pl.BlockSpec(memory_space=pltpu.VMEM)
    sem = pltpu.SemaphoreType.DMA
    outs = pl.pallas_call(
        functools.partial(kernel, n, lat, cols),
        out_shape=(
            jax.ShapeDtypeStruct((cells, chans), BF),
            jax.ShapeDtypeStruct((cells, chans), BF),
            jax.ShapeDtypeStruct((chans // n, hid), F32),
            jax.ShapeDtypeStruct((hid // n, chans), F32),
            jax.ShapeDtypeStruct(depth_kernel.shape, F32),
            jax.ShapeDtypeStruct((1, chans), F32),
            jax.ShapeDtypeStruct((1, chans), F32),
        ),
        in_specs=[pl.BlockSpec(memory_space=pltpu.SMEM)] + [vm] * 8 + [pl.BlockSpec(memory_space=pl.ANY)] * 2,
        out_specs=(vm,) * 7,
        scratch_shapes=[
            pltpu.VMEM((chans, hid), BF),
            pltpu.VMEM((hid, chans), BF),
            pltpu.VMEM((depth, chans), BF),
            pltpu.VMEM((depth, chans), BF),
            pltpu.VMEM((6 * lat, chans), BF),
            pltpu.VMEM((6 * lat, chans), BF),
            pltpu.VMEM((n, 6 * cols, chans // 2), BF),
            pltpu.VMEM((n, 6 * cols, chans // 2), BF),
            pltpu.VMEM((7, lat + 6, cols, chans), F32),
            pltpu.VMEM((7, lat + 6, cols, chans), F32),
            pltpu.VMEM((7, 3, cols, chans), F32),
            pltpu.VMEM((cells, chans), F32),
            pltpu.VMEM((cells, chans), BF),
            pltpu.VMEM((cells, 1), F32),
            pltpu.VMEM((cells, chans), BF),
            pltpu.VMEM((cells, chans), F32),
            pltpu.VMEM((cells, chans), F32),
            pltpu.VMEM((cells, chans), F32),
            pltpu.VMEM((rows, TILE), F32),
            pltpu.VMEM((rows, TILE), F32),
            pltpu.VMEM((rows, TILE), BF),
            pltpu.VMEM((rows, TILE), BF),
            pltpu.VMEM((rows, TILE), BF),
            pltpu.VMEM((rows, TILE), BF),
            pltpu.VMEM((logn + 1, 56, chans), F32),
            pltpu.VMEM((logn, 56, chans), F32),
            sem((2,)),
            sem((4,)),
            sem((4,)),
            sem((2 * n,)),
            sem((2 * n,)),
            sem((logn,)),
            sem((logn,)),
            sem((logn,)),
            sem((logn,)),
            sem((logn,)),
            sem((logn,)),
        ],
        compiler_params=pltpu.CompilerParams(
            collective_id=0, has_side_effects=True, vmem_limit_bytes=52 * 1024 * 1024
        ),
    )(
        fold_partner,
        state_in.reshape(cells, chans),
        ocean_mask.astype(F32).reshape(cells, 1),
        depth_kernel,
        norm_gain.reshape(1, chans),
        norm_bias.reshape(1, chans),
        cotangent.reshape(cells, chans),
        jnp.asarray(shifts, BF),
        jnp.asarray(packs, BF),
        w_up,
        w_down,
    )
    out, gstate, gup, gdn, gk, ggain, gbias = outs
    return (
        out.reshape(lat, cols, chans),
        gstate.reshape(lat, cols, chans),
        gup,
        gdn,
        gk,
        ggain.reshape(chans),
        gbias.reshape(chans),
    )


def solution(mesh):
    return jax.shard_map(
        on_device,
        mesh=mesh,
        in_specs=(
            P("ens", "lon", None),
            P(None, "lon"),
            P(),
            P(),
            P(),
            P(),
            P(),
            P(),
            P("ens", "lon", None),
        ),
        out_specs=(
            P("ens", "lon", None),
            P("ens", "lon", None),
            P(("ens", "lon"), None),
            P(("ens", "lon"), None),
            P("ens", None),
            P("ens"),
            P("ens"),
        ),
        check_vma=False,
    )
```

time: 307 us -> 81.6 us (0.27)
  waiting for transfers between devices: 148 us -> 0 us
  blocking collectives: 74.2 us -> 0 us
  Pallas kernels: 0 us -> 68.7 us
  matrix products: 31.2 us -> 0 us
  other arithmetic: 14.5 us -> 0.69 us
  between operations: 14.1 us -> 0.67 us
  starting transfers between devices: 10.1 us -> 0 us
    reduce_scatter x2 -> x0, waiting for transfers between devices: 119 us -> none  [the longest x1 74.1 us: on_device(): lax.psum_scatter(lax.dot_general(part_norm, grad_pre, (((0,), (0,)), ((),...]
    pallas_call x0 -> x1, Pallas kernels: none -> 68.7 us  [on_device(): pl.pallas_call(functools.partial(kernel, n, lat, cols), out_shape=(jax.Sh...]
    all_gather x2 -> x0, blocking collectives: 44.1 us -> none  [the longest x1 23.7 us: on_device(): lax.all_gather(north_grad.astype(jnp.bfloat16), 'lon', axis=1, tiled=True)]
    psum x1 -> x0, blocking collectives: 30.1 us -> none  [on_device(): gain_sum, bias_sum = lax.psum((gain_part, bias_part), 'lon')]
    psum x1 -> x0, waiting for transfers between devices: 29.4 us -> none  [on_device(): kernel_sum = lax.psum(kernel_part, 'lon')]
    conv_general_dilated x2 -> x0, matrix products: 14.1 us -> none  [depth_conv(): lax.conv_general_dilated(extended[None], depth_kernel.reshape(7, 7, 1, ch...]
    dot_general x6 -> x0, matrix products: 13.3 us -> none  [the longest x1 3.79 us: on_device(): lax.dot_general(part_norm, grad_pre, (((0,), (0,)), ((), ())), preferred_...]
    ppermute x4 -> x0, starting transfers between devices: 10 us -> none  [the longest x2 9.15 us: with_halo(): lax.ppermute(head, axis, [((i + 1) % count, i) for i in range(count)])]
  transfers between devices with their start and end apart: 7 -> 0, of which waited for: 3 -> 0; matrix products, arithmetic and copies ran while one was open for 11% -> 0% of each run, Pallas kernels for 0% -> 0%
where the time goes in v1:
time: 81.6 us; the launch traced here: 81.2 us
  Pallas kernels  68.7 us (84%)
  local copies, waits for them, and re-layouts  11.1 us (14%)
    pallas_call x1, Pallas kernels, on_device(): pl.pallas_call(functools.partial(kernel, n, lat, cols), out_shape=(jax.Sh...  68.7 us
    unnamed x23, local copies, waits for them, and re-layouts  11 us

profile of v1, /device:TPU:0, one launch (start us, length us, event | category | flops | bytes accessed | tf_op | source)
XLA Modules:
  0.0 81.2 jit_solution(3259234222491374375)
XLA Ops:
  0.6 0.7 convert_element_type.3
  1.3 0.1 copy.20
  1.4 0.1 reshape.50.mask_ref
  1.5 0.0 copy-start
  1.5 1.0 %copy-done = bf16[896,256]{1,0:T(8,128)(2,1)S(1)} copy-done((bf16[896,256]{1,0:T(8,128)(2,1)S(1)}, bf16[896,256]{1,0:T(8,128)(2,1)}, u32[]{:S(2)}) %copy-start) | copy-done | bytes 458776
  2.5 0.0 copy-start.1
  2.5 0.9 %copy-done.1 = bf16[16,8,512]{2,1,0:T(8,128)(2,1)S(1)} copy-done((bf16[16,8,512]{2,1,0:T(8,128)(2,1)S(1)}, bf16[16,8,512]{2,1,0:T(8,128)(2,1)}, u32[]{:S(2)}) %copy-start.1) | copy-done | bytes 131096
  3.4 0.0 copy-start.2
  3.4 0.9 %copy-done.2 = bf16[16,8,512]{2,1,0:T(8,128)(2,1)S(1)} copy-done((bf16[16,8,512]{2,1,0:T(8,128)(2,1)S(1)}, bf16[16,8,512]{2,1,0:T(8,128)(2,1)}, u32[]{:S(2)}) %copy-start.2) | copy-done | bytes 131096
  4.3 0.0 copy-start.3
  4.3 0.9 %copy-done.3 = f32[49,512]{1,0:T(8,128)S(1)} copy-done((f32[49,512]{1,0:T(8,128)S(1)}, f32[49,512]{1,0:T(8,128)}, u32[]{:S(2)}) %copy-start.3) | copy-done | bytes 100376
  5.2 0.0 copy-start.4
  5.2 0.7 copy-done.4
  6.0 0.0 copy-start.5
  6.0 0.7 copy-done.5
  6.6 0.0 copy-start.6
  6.6 0.7 copy-done.6
  7.3 0.0 copy-start.7
  7.3 0.7 copy-done.7
  8.0 68.7 %shard_map.162 = (bf16[128,512]{1,0:T(8,128)(2,1)S(1)}, bf16[128,512]{1,0:T(8,128)(2,1)S(1)}, f32[32,2048]{1,0:T(8,128)S(1)}, f32[128,512]{1,0:T(8,128)S(1)}, f3...) custom-call(s32[128]{0:T(128)S(1)} %copy-done.7, bf16[128,512]{1,0:T(8,128)(2,1)S(1)} %bitcast.8, ...), custom_call_target="tpu_custom_call" | custom-call | tf_op jit(solution)/shard_map/pallas_call | solution.py:402
  76.7 0.7 copy.29
  77.3 0.7 copy.30
  78.0 0.7 copy.31
  78.7 0.7 copy.32
  79.4 0.6 copy.33
  80.1 0.6 copy.34
  80.6 0.6 copy.35
Async XLA Ops:
  1.5 1.0 %copy-start = (bf16[896,256]{1,0:T(8,128)(2,1)S(1)}, bf16[896,256]{1,0:T(8,128)(2,1)}, u32[]{:S(2)}) copy-start(bf16[896,256]{1,0:T(8,128)(2,1)} %constant.4.clone.shift_ref) | copy-start | bytes 1376260
  2.5 0.9 %copy-start.1 = (bf16[16,8,512]{2,1,0:T(8,128)(2,1)S(1)}, bf16[16,8,512]{2,1,0:T(8,128)(2,1)}, u32[]{:S(2)}) copy-start(bf16[16,8,512]{2,1,0:T(8,128)(2,1)} %param.11) | copy-start | bytes 393220
  3.4 0.9 %copy-start.2 = (bf16[16,8,512]{2,1,0:T(8,128)(2,1)S(1)}, bf16[16,8,512]{2,1,0:T(8,128)(2,1)}, u32[]{:S(2)}) copy-start(bf16[16,8,512]{2,1,0:T(8,128)(2,1)} %param.19) | copy-start | bytes 393220
  4.3 0.9 %copy-start.3 = (f32[49,512]{1,0:T(8,128)S(1)}, f32[49,512]{1,0:T(8,128)}, u32[]{:S(2)}) copy-start(f32[49,512]{1,0:T(8,128)} %dk_ref.1) | copy-start | bytes 301060
  5.2 0.7 copy-start.4
  6.0 0.7 copy-start.5
  6.6 0.7 copy-start.6
  7.3 0.7 copy-start.7

commit v2 on v1

--- a/solution.py
+++ b/solution.py
@@ -11,6 +11,7 @@
 
 EPS = 1e-06
 TILE = 512
+LANES = 256
 BF = jnp.bfloat16
 F32 = jnp.float32
 GELU_A = math.sqrt(2.0 / math.pi)
@@ -53,10 +54,10 @@
 
 def kernel(
     n, lat, cols,
-    fold_ref, state_ref, mask_ref, dk_ref, gain_ref, bias_ref, cot_ref, shift_ref, pack_ref, wup_hbm, wdn_hbm,
+    fold_ref, state_hbm, mask_hbm, pack_hbm, shift_hbm, dk_hbm, gain_hbm, bias_hbm, cot_hbm, wup_hbm, wdn_hbm,
     out_ref, gstate_ref, gup_ref, gdn_ref, gk_ref, ggain_ref, gbias_ref,
-    wup, wdn, ext, ext_g, pk, pk_g, top, top_g, sh, sh_g, sh_f, norm_s, nout_s, inv_s, ups, br, gn, gc,
-    acc_d, acc_u, snd_d, snd_u, rcv_d, rcv_u, smb, smr,
+    state_ref, mask_ref, pack_ref, shift_ref, dk_ref, gain_ref, bias_ref, cot_ref, wup, wdn, ext, ext_g, pk, pk_g, top, top_g, sh, sh_g, sh_f, norm_s, nout_s, inv_s, ups, br, gn, gc,
+    acc_d, acc_u, snd_d, snd_u, rcv_d, rcv_u, sm, sm_r, cur, cur_r, sums_s,
     w_sem, h_send, h_recv, t_send, t_recv, d_send, d_recv, u_send, u_recv, s_send, s_recv,
 ):
     chans = state_ref.shape[1]
@@ -71,11 +72,14 @@
     right, left = (me + 1) % n, (me + n - 1) % n
     half_c = chans // 2
 
-    w_copies = [
-        pltpu.make_async_copy(wup_hbm, wup, w_sem.at[0]),
-        pltpu.make_async_copy(wdn_hbm, wdn, w_sem.at[1]),
+    loads = [
+        pltpu.make_async_copy(src, dst, w_sem.at[i])
+        for i, (src, dst) in enumerate((
+            (state_hbm, state_ref), (mask_hbm, mask_ref), (pack_hbm, pack_ref), (shift_hbm, shift_ref),
+            (dk_hbm, dk_ref), (gain_hbm, gain_ref), (bias_hbm, bias_ref), (cot_hbm, cot_ref),
+            (wup_hbm, wup), (wdn_hbm, wdn)))
     ]
-    for c in w_copies:
+    for c in loads:
         c.start()
 
     barrier = pltpu.get_barrier_semaphore()
@@ -84,6 +88,8 @@
     def _(k):
         pl.semaphore_signal(barrier, inc=1, device_id={"lon": (me + k) % n}, device_id_type=pl.DeviceIdType.MESH)
 
+    for c in loads[:3]:
+        c.wait()
     mask = mask_ref[...]
     mask_bf = mask.astype(BF)
 
@@ -101,8 +107,16 @@
             remote(p_ref.at[pl.ds(0, edge)], e_ref.at[pl.ds(right0, edge)], h_send.at[2 * w + 1], h_recv.at[2 * w + 1], left),
         ]
 
+    mine, pairs = me % 2, n // 2
+
     def top_copy(t_ref, w, k):
-        return remote(t_ref.at[me], t_ref.at[me], t_send.at[w * n + k], t_recv.at[w * n + k], (me + k) % n)
+        block = t_ref.at[mine, me // 2]
+        at = w * (pairs + 1) + k
+        return remote(block, block, t_send.at[at], t_recv.at[at], (me + 2 * k) % n)
+
+    def pair_copy(t_ref, w):
+        at = w * (pairs + 1) + pairs
+        return remote(t_ref.at[mine], t_ref.at[mine], t_send.at[at], t_recv.at[at], me + 1 - 2 * mine)
 
     def prepare(e_ref, p_ref, t_ref, values_bf):
         e_ref[pl.ds(own0, cells), :] = values_bf
@@ -111,14 +125,14 @@
         p_ref[...] = dot(pack_ref[...], values_bf).astype(BF)
         for k in range(3):
             row = values_bf[(lat - 3 + k) * cols:(lat - 2 + k) * cols].astype(F32)
-            t_ref[me, pl.ds(k * 2 * cols, 2 * cols), :] = jnp.concatenate(
+            t_ref[mine, me // 2, pl.ds(k * 2 * cols, 2 * cols), :] = jnp.concatenate(
                 [row[:, :half_c], row[:, half_c:]], axis=0).astype(BF)
 
     def send_all(e_ref, p_ref, t_ref, w):
         for c in halo_copies(e_ref, p_ref, w):
             c.start()
 
-        @pl.loop(1, n)
+        @pl.loop(1, pairs)
         def _(k):
             top_copy(t_ref, w, k).start()
 
@@ -126,10 +140,15 @@
         for c in halo_copies(e_ref, p_ref, w):
             c.wait_recv()
 
-    def wait_top(t_ref, w):
-        @pl.loop(1, n)
+    def pass_top(t_ref, w):
+        @pl.loop(1, pairs)
         def _(k):
             top_copy(t_ref, w, k).wait_recv()
+
+        pair_copy(t_ref, w).start()
+
+    def wait_top(t_ref, w):
+        pair_copy(t_ref, w).wait_recv()
 
     def put_shifts(e_ref, s_ref):
         s_ref[:, pl.ds(0, 3)] = jnp.zeros((7, 3, cols, chans), F32)
@@ -139,7 +158,7 @@
 
     def put_fold(t_ref, sel, store):
         for k in range(3):
-            rows = t_ref[:, pl.ds(k * 2 * cols, 2 * cols), :].reshape(n * 2 * cols, half_c)
+            rows = t_ref[:, :, pl.ds(k * 2 * cols, 2 * cols), :].reshape(n * 2 * cols, half_c)
             got = dot(sel, rows).reshape(2, 7, cols, half_c)
             for h in range(2):
                 for b in range(7):
@@ -161,16 +180,20 @@
     want = jnp.where(want < 0, want + total, want)
     want = jnp.where(want < 0, want + total, want)
     want = jnp.where(want >= total, want - total, want)
-    have = (q_id // (2 * cols)) * cols + q_id % cols
+    slot = q_id // (2 * cols)
+    have = (2 * (slot % pairs) + slot // pairs) * cols + q_id % cols
     half_q = (q_id // cols) % 2
     sel = jnp.where((have == want) & (half_q == half_m), 1.0, 0.0).astype(BF)
 
+    for c in loads[3:8]:
+        c.wait()
     cot = cot_ref[...]
     upstream = cot * mask_bf
     ups[...] = upstream
 
     wait_halo(ext, pk, 0)
     put_shifts(ext, sh)
+    pass_top(top, 0)
     wait_top(top, 0)
 
     def store_north(k, b, ls, val):
@@ -196,7 +219,7 @@
     normed = centred * inv
     norm_s[...] = normed
     nout_s[...] = (normed * gain_ref[...] + bias_ref[...]).astype(BF)
-    for c in w_copies:
+    for c in loads[8:]:
         c.wait()
     br[...] = jnp.zeros_like(br)
     gn[...] = jnp.zeros_like(gn)
@@ -242,37 +265,49 @@
             base = base + bit_of(order[k]) * (size >> (k + 1))
         return base
 
-    def rs_copy(snd, rcv, ss, rs, order, s):
-        off, half = size - (size >> s), size >> (s + 1)
-        return remote(snd.at[pl.ds(off, half)], rcv.at[pl.ds(off, half)], ss.at[s], rs.at[s], partner(order[s]))
-
-    def rs_send(acc, snd, rcv, ss, rs, order, s):
+    def rs_copy(part, h, s):
+        acc, snd, rcv, ss, rs, order = part
+        at = pl.ds(size - (size >> s), size >> (s + 1))
+        sem = h * logn + s
+        return remote(snd.at[h, at], rcv.at[h, at], ss.at[sem], rs.at[sem], partner(order[s]))
+
+    def rs_send(part, h, s):
+        acc, snd, rcv, ss, rs, order = part
         off, half = size - (size >> s), size >> (s + 1)
         base = rs_base(order, s) + (1 - bit_of(order[s])) * half
-        blk = min(64, half)
+        blk = min(128, half)
 
         @pl.loop(0, half // blk)
         def _(i):
-            snd[pl.ds(pl.multiple_of(off + i * blk, 16), blk), :] = acc[
-                pl.ds(pl.multiple_of(base + i * blk, 16), blk), :].astype(BF)
-
-        rs_copy(snd, rcv, ss, rs, order, s).start()
-
-    def rs_recv(acc, snd, rcv, ss, rs, order, s):
+            snd[h, pl.ds(pl.multiple_of(off + i * blk, 16), blk), :] = acc[
+                pl.ds(pl.multiple_of(base + i * blk, 16), blk), pl.ds(h * LANES, LANES)].astype(BF)
+
+        rs_copy(part, h, s).start()
+
+    def rs_recv(part, h, s):
+        acc, snd, rcv, ss, rs, order = part
         off, half = size - (size >> s), size >> (s + 1)
         base = rs_base(order, s + 1)
-        blk = min(64, half)
-        rs_copy(snd, rcv, ss, rs, order, s).wait_recv()
+        blk = min(128, half)
+        rs_copy(part, h, s).wait_recv()
 
         @pl.loop(0, half // blk)
         def _(i):
             at = pl.ds(pl.multiple_of(base + i * blk, 16), blk)
-            acc[at, :] += rcv[pl.ds(pl.multiple_of(off + i * blk, 16), blk), :].astype(F32)
+            acc[at, pl.ds(h * LANES, LANES)] += rcv[h, pl.ds(pl.multiple_of(off + i * blk, 16), blk), :].astype(F32)
+
+    def rs_next(h, s):
+        for part in (down, upw):
+            rs_recv(part, h, s)
+            if s + 1 < logn:
+                rs_send(part, h, s + 1)
 
     down = (acc_d, snd_d, rcv_d, d_send, d_recv, order_d)
     upw = (acc_u, snd_u, rcv_u, u_send, u_recv, order_u)
-    rs_send(*down, 0)
-    rs_send(*upw, 0)
+    halves = TILE // LANES
+    for h in range(halves):
+        rs_send(down, h, 0)
+        rs_send(upw, h, 0)
 
     gnorm = gn[...]
     normed = norm_s[...]
@@ -288,16 +323,15 @@
     prepare(ext_g, pk_g, top_g, grad_conv.astype(BF))
     send_all(ext_g, pk_g, top_g, 1)
     taps = dk_ref.shape[0]
-    smb[0, pl.ds(48, 8), :] = jnp.zeros((8, chans), F32)
-    smb[0, pl.ds(taps, 1), :] = gain_row
-    smb[0, pl.ds(taps + 1, 1), :] = bias_row
+    for ct in range(chans // 128):
+        sm[ct, pl.ds(48, 8), :] = jnp.zeros((8, 128), F32)
+        sm[ct, pl.ds(taps, 1), :] = gain_row[:, ct * 128:(ct + 1) * 128]
+        sm[ct, pl.ds(taps + 1, 1), :] = bias_row[:, ct * 128:(ct + 1) * 128]
 
     out_ref[...] = (state_ref[...].astype(F32) + mask * br[...]).astype(BF)
 
-    rs_recv(*down, 0)
-    rs_send(*down, 1)
-    rs_recv(*upw, 0)
-    rs_send(*upw, 1)
+    for h in range(halves):
+        rs_next(h, 0)
 
     @pl.loop(0, chans // 128)
     def _(ct):
@@ -307,15 +341,38 @@
             window = sh[b, :, :, ls]
             for a in range(7):
                 part = jnp.sum(g * window[a:a + lat], axis=0)
-                smb[0, pl.ds(7 * a + b, 1), ls] = jnp.sum(part, axis=0, keepdims=True)
+                sm[ct, pl.ds(7 * a + b, 1), :] = jnp.sum(part, axis=0, keepdims=True)
+
+    quarters = chans // 512
+    b0, b1 = bit_of(0), bit_of(1)
+    keep0, send0 = pl.ds(2 * quarters * b0, 2 * quarters), pl.ds(2 * quarters * (1 - b0), 2 * quarters)
+    keep1 = pl.ds(quarters * (2 * b0 + b1), quarters)
+    send1 = pl.ds(quarters * (2 * b0 + 1 - b1), quarters)
 
     def sm_copy(s):
-        return remote(smb.at[s], smr.at[s], s_send.at[s], s_recv.at[s], partner(s))
+        if s == 0:
+            src, dst, bit = sm.at[send0], sm_r.at[pl.ds(0, 2 * quarters)], 0
+        elif s == 1:
+            src, dst, bit = sm.at[send1], sm_r.at[pl.ds(2 * quarters, quarters)], 1
+        elif s < logn:
+            src, dst, bit = cur.at[s], cur_r.at[s], s
+        elif s == logn:
+            src, dst, bit = sums_s.at[keep1], sums_s.at[keep1], 1
+        else:
+            src, dst, bit = sums_s.at[keep0], sums_s.at[keep0], 0
+        return remote(src, dst, s_send.at[s], s_recv.at[s], partner(bit))
 
     def sm_step(s):
         sm_copy(s).wait_recv()
-        smb[s + 1] = smb[s] + smr[s]
-        if s + 1 < logn:
+        if s == 0:
+            sm[keep0] = sm[keep0] + sm_r[pl.ds(0, 2 * quarters)]
+        elif s == 1:
+            cur[2] = sm[keep1] + sm_r[pl.ds(2 * quarters, quarters)]
+        elif s < logn - 1:
+            cur[s + 1] = cur[s] + cur_r[s]
+        elif s == logn - 1:
+            sums_s[keep1] = cur[s] + cur_r[s]
+        if s < logn + 1:
             sm_copy(s + 1).start()
 
     sm_copy(0).start()
@@ -324,6 +381,8 @@
     put_shifts(ext_g, sh_g)
     sh_g[:, pl.ds(lat + 3, 3)] = jnp.zeros((7, 3, cols, chans), F32)
     sm_step(0)
+    pass_top(top_g, 1)
+    sm_step(1)
     wait_top(top_g, 1)
 
     def store_facing(k, b, ls, val):
@@ -354,13 +413,13 @@
 
     gstate_ref[...] = (cot_ref[...].astype(F32) + mask * gc[...]).astype(BF)
 
+    steps = list(range(2, logn + 2))
     for s in range(1, logn):
-        rs_recv(*down, s)
-        if s + 1 < logn:
-            rs_send(*down, s + 1)
-        rs_recv(*upw, s)
-        if s + 1 < logn:
-            rs_send(*upw, s + 1)
+        for h in range(halves):
+            rs_next(h, s)
+            if steps:
+                sm_step(steps.pop(0))
+    for s in steps:
         sm_step(s)
 
     base_d = pl.multiple_of(rs_base(order_d, logn), 8)
@@ -368,22 +427,34 @@
     gdn_ref[...] = acc_d[pl.ds(base_d, rows_d), :] * scale
     for t in range(hid // TILE):
         gup_ref[:, pl.ds(t * TILE, TILE)] = acc_u[pl.ds(pl.multiple_of(base_u + t * rows_u, 8), rows_u), :] * scale
-    gk_ref[...] = smb[logn, pl.ds(0, taps), :] * scale
-    ggain_ref[...] = smb[logn, pl.ds(taps, 1), :] * scale
-    gbias_ref[...] = smb[logn, pl.ds(taps + 1, 1), :] * scale
+    for ct in range(chans // 128):
+        ls = pl.ds(ct * 128, 128)
+        gk_ref[:, ls] = sums_s[ct, pl.ds(0, taps), :] * scale
+        ggain_ref[:, ls] = sums_s[ct, pl.ds(taps, 1), :] * scale
+        gbias_ref[:, ls] = sums_s[ct, pl.ds(taps + 1, 1), :] * scale
 
     for e_ref, p_ref, t_ref, w in ((ext, pk, top, 0), (ext_g, pk_g, top_g, 1)):
         for c in halo_copies(e_ref, p_ref, w):
             c.wait_send()
 
-        @pl.loop(1, n)
+        @pl.loop(1, pairs)
         def _(k):
             top_copy(t_ref, w, k).wait_send()
 
+        pair_copy(t_ref, w).wait_send()
+
     for s in range(logn):
-        rs_copy(*down[1:], s).wait_send()
-        rs_copy(*upw[1:], s).wait_send()
+        for h in range(halves):
+            rs_copy(down, h, s).wait_send()
+            rs_copy(upw, h, s).wait_send()
+    for s in range(logn + 2):
         sm_copy(s).wait_send()
+
+
+def finish(*refs):
+    count = len(refs) // 2
+    for src, dst in zip(refs[:count], refs[count:]):
+        dst[...] = src[...]
 
 
 def on_device(
@@ -398,6 +469,7 @@
     depth = shifts.shape[1]
     rows = hid * chans // TILE
     vm = pl.BlockSpec(memory_space=pltpu.VMEM)
+    hbm = pl.BlockSpec(memory_space=pl.ANY)
     sem = pltpu.SemaphoreType.DMA
     outs = pl.pallas_call(
         functools.partial(kernel, n, lat, cols),
@@ -410,17 +482,25 @@
             jax.ShapeDtypeStruct((1, chans), F32),
             jax.ShapeDtypeStruct((1, chans), F32),
         ),
-        in_specs=[pl.BlockSpec(memory_space=pltpu.SMEM)] + [vm] * 8 + [pl.BlockSpec(memory_space=pl.ANY)] * 2,
+        in_specs=[pl.BlockSpec(memory_space=pltpu.SMEM)] + [hbm] * 10,
         out_specs=(vm,) * 7,
         scratch_shapes=[
+            pltpu.VMEM((cells, chans), BF),
+            pltpu.VMEM((cells, 1), F32),
+            pltpu.VMEM(packs.shape, BF),
+            pltpu.VMEM(shifts.shape, BF),
+            pltpu.VMEM(depth_kernel.shape, F32),
+            pltpu.VMEM((1, chans), F32),
+            pltpu.VMEM((1, chans), F32),
+            pltpu.VMEM((cells, chans), BF),
             pltpu.VMEM((chans, hid), BF),
             pltpu.VMEM((hid, chans), BF),
             pltpu.VMEM((depth, chans), BF),
             pltpu.VMEM((depth, chans), BF),
             pltpu.VMEM((6 * lat, chans), BF),
             pltpu.VMEM((6 * lat, chans), BF),
-            pltpu.VMEM((n, 6 * cols, chans // 2), BF),
-            pltpu.VMEM((n, 6 * cols, chans // 2), BF),
+            pltpu.VMEM((2, n // 2, 6 * cols, chans // 2), BF),
+            pltpu.VMEM((2, n // 2, 6 * cols, chans // 2), BF),
             pltpu.VMEM((7, lat + 6, cols, chans), F32),
             pltpu.VMEM((7, lat + 6, cols, chans), F32),
             pltpu.VMEM((7, 3, cols, chans), F32),
@@ -433,41 +513,49 @@
             pltpu.VMEM((cells, chans), F32),
             pltpu.VMEM((rows, TILE), F32),
             pltpu.VMEM((rows, TILE), F32),
-            pltpu.VMEM((rows, TILE), BF),
-            pltpu.VMEM((rows, TILE), BF),
-            pltpu.VMEM((rows, TILE), BF),
-            pltpu.VMEM((rows, TILE), BF),
-            pltpu.VMEM((logn + 1, 56, chans), F32),
-            pltpu.VMEM((logn, 56, chans), F32),
-            sem((2,)),
+            pltpu.VMEM((TILE // LANES, rows, LANES), BF),
+            pltpu.VMEM((TILE // LANES, rows, LANES), BF),
+            pltpu.VMEM((TILE // LANES, rows, LANES), BF),
+            pltpu.VMEM((TILE // LANES, rows, LANES), BF),
+            pltpu.VMEM((chans // 128, 56, 128), F32),
+            pltpu.VMEM((3 * chans // 512, 56, 128), F32),
+            pltpu.VMEM((logn, chans // 512, 56, 128), F32),
+            pltpu.VMEM((logn, chans // 512, 56, 128), F32),
+            pltpu.VMEM((chans // 128, 56, 128), F32),
+            sem((10,)),
             sem((4,)),
             sem((4,)),
-            sem((2 * n,)),
-            sem((2 * n,)),
-            sem((logn,)),
-            sem((logn,)),
-            sem((logn,)),
-            sem((logn,)),
-            sem((logn,)),
-            sem((logn,)),
+            sem((n + 2,)),
+            sem((n + 2,)),
+            sem((TILE // LANES * logn,)),
+            sem((TILE // LANES * logn,)),
+            sem((TILE // LANES * logn,)),
+            sem((TILE // LANES * logn,)),
+            sem((logn + 2,)),
+            sem((logn + 2,)),
         ],
         compiler_params=pltpu.CompilerParams(
-            collective_id=0, has_side_effects=True, vmem_limit_bytes=52 * 1024 * 1024
+            collective_id=0, has_side_effects=True, vmem_limit_bytes=64 * 1024 * 1024
         ),
     )(
         fold_partner,
         state_in.reshape(cells, chans),
         ocean_mask.astype(F32).reshape(cells, 1),
+        jnp.asarray(packs, BF),
+        jnp.asarray(shifts, BF),
         depth_kernel,
         norm_gain.reshape(1, chans),
         norm_bias.reshape(1, chans),
         cotangent.reshape(cells, chans),
-        jnp.asarray(shifts, BF),
-        jnp.asarray(packs, BF),
         w_up,
         w_down,
     )
-    out, gstate, gup, gdn, gk, ggain, gbias = outs
+    out, gstate, gup, gdn, gk, ggain, gbias = pl.pallas_call(
+        finish,
+        out_shape=tuple(jax.ShapeDtypeStruct(o.shape, o.dtype) for o in outs),
+        in_specs=[vm] * 7,
+        out_specs=(vm,) * 7,
+    )(*outs)
     return (
         out.reshape(lat, cols, chans),
         gstate.reshape(lat, cols, chans),

time: 81.6 us -> 63.9 us (0.78)
  local copies, waits for them, and re-layouts: 11.1 us -> 0.79 us
  Pallas kernels: 68.7 us -> 61.6 us
    unnamed x23 -> x0, local copies, waits for them, and re-layouts: 11 us -> none
    pallas_call x1, Pallas kernels: 68.7 us -> 59.4 us  [on_device(): pl.pallas_call(functools.partial(kernel, n, lat, cols), out_shape=(jax.Sh...]
    pallas_call x0 -> x1, Pallas kernels: none -> 2.12 us  [on_device(): pl.pallas_call(finish, out_shape=tuple((jax.ShapeDtypeStruct(o.shape, o.d...]
where the time goes in v2:
time: 63.9 us; the launch traced here: 63.7 us
  Pallas kernels  61.6 us (96%)
  local copies, waits for them, and re-layouts  0.79 us (1%)
  other arithmetic  0.69 us (1%)
  between operations  0.64 us (1%)
    pallas_call x1, Pallas kernels, on_device(): pl.pallas_call(functools.partial(kernel, n, lat, cols), out_shape=(jax.Sh...  59.4 us
    pallas_call x1, Pallas kernels, on_device(): pl.pallas_call(finish, out_shape=tuple((jax.ShapeDtypeStruct(o.shape, o.d...  2.12 us

profile of v2, /device:TPU:0, one launch (start us, length us, event | category | flops | bytes accessed | tf_op | source)
XLA Modules:
  0.0 63.7 jit_solution(4532714146907022498)
XLA Ops:
  0.6 0.7 %convert_element_type.3 = f32[16,8]{0,1:T(8,128)S(1)} convert(s32[16,8]{0,1:T(8,128)} %param.12) | non-fusion elementwise | flops 128 | bytes 1024 | tf_op jit(solution)/shard_map/convert_element_type | solution.py:543
  1.3 0.1 copy.20
  1.4 0.7 %reshape.50.mask_hbm = f32[128,1]{1,0:T(8,128)} reshape(f32[16,8]{1,0:T(8,128)S(1)} %copy.20) | data formatting | bytes 1024 | tf_op jit(solution)/shard_map/reshape | solution.py:543
  2.1 59.4 %shard_map.162 = (bf16[128,512]{1,0:T(8,128)(2,1)}, bf16[128,512]{1,0:T(8,128)(2,1)}, f32[32,2048]{1,0:T(8,128)}, f32[128,512]{1,0:T(8,128)}, f32[49,512]{1,0:T(...) custom-call(s32[128]{0:T(128)} %fold_ref.1, bf16[128,512]{1,0:T(8,128)(2,1)} %bitcast.8, f32[128,1]{1,0:T(8,128)} %reshape.50.mask_hbm, ...), custom_call_target="tpu_custom_call" | custom-call | tf_op jit(solution)/shard_map/pallas_call | solution.py:474
  61.6 2.1 %shard_map.163 = (bf16[128,512]{1,0:T(8,128)(2,1)}, bf16[128,512]{1,0:T(8,128)(2,1)}, f32[32,2048]{1,0:T(8,128)}, f32[128,512]{1,0:T(8,128)}, f32[49,512]{1,0:T(...) custom-call(bf16[128,512]{1,0:T(8,128)(2,1)} %get-tuple-element.21.refs_0_, bf16[128,512]{1,0:T(8,128)(2,1)} %get-tuple-element.22.refs_1_, ...), custom_call_target="tpu_custom_call" | custom-call | tf_op jit(solution)/shard_map/pallas_call | solution.py:553

commit v3 on v2

--- a/solution.py
+++ b/solution.py
@@ -328,10 +328,10 @@
         sm[ct, pl.ds(taps, 1), :] = gain_row[:, ct * 128:(ct + 1) * 128]
         sm[ct, pl.ds(taps + 1, 1), :] = bias_row[:, ct * 128:(ct + 1) * 128]
 
-    out_ref[...] = (state_ref[...].astype(F32) + mask * br[...]).astype(BF)
-
     for h in range(halves):
         rs_next(h, 0)
+
+    out_ref[...] = (state_ref[...].astype(F32) + mask * br[...]).astype(BF)
 
     @pl.loop(0, chans // 128)
     def _(ct):

time: 63.9 us -> 63.9 us (level)
  no operation moved by 1% of the time
where the time goes in v3:
time: 63.9 us; the launch traced here: 63.7 us
  Pallas kernels  61.6 us (96%)
  local copies, waits for them, and re-layouts  0.79 us (1%)
  other arithmetic  0.69 us (1%)
  between operations  0.64 us (1%)
    pallas_call x1, Pallas kernels, on_device(): pl.pallas_call(functools.partial(kernel, n, lat, cols), out_shape=(jax.Sh...  59.4 us
    pallas_call x1, Pallas kernels, on_device(): pl.pallas_call(finish, out_shape=tuple((jax.ShapeDtypeStruct(o.shape, o.d...  2.12 us

profile of v3, /device:TPU:0, one launch (start us, length us, event | category | flops | bytes accessed | tf_op | source)
XLA Modules:
  0.0 63.7 jit_solution(5503032641396546578)
XLA Ops:
  0.6 0.7 %convert_element_type.3 = f32[16,8]{0,1:T(8,128)S(1)} convert(s32[16,8]{0,1:T(8,128)} %param.12) | non-fusion elementwise | flops 128 | bytes 1024 | tf_op jit(solution)/shard_map/convert_element_type | solution.py:543
  1.3 0.1 copy.20
  1.4 0.7 %reshape.50.mask_hbm = f32[128,1]{1,0:T(8,128)} reshape(f32[16,8]{1,0:T(8,128)S(1)} %copy.20) | data formatting | bytes 1024 | tf_op jit(solution)/shard_map/reshape | solution.py:543
  2.1 59.4 %shard_map.162 = (bf16[128,512]{1,0:T(8,128)(2,1)}, bf16[128,512]{1,0:T(8,128)(2,1)}, f32[32,2048]{1,0:T(8,128)}, f32[128,512]{1,0:T(8,128)}, f32[49,512]{1,0:T(...) custom-call(s32[128]{0:T(128)} %fold_ref.1, bf16[128,512]{1,0:T(8,128)(2,1)} %bitcast.8, f32[128,1]{1,0:T(8,128)} %reshape.50.mask_hbm, ...), custom_call_target="tpu_custom_call" | custom-call | tf_op jit(solution)/shard_map/pallas_call | solution.py:474
  61.6 2.1 %shard_map.163 = (bf16[128,512]{1,0:T(8,128)(2,1)}, bf16[128,512]{1,0:T(8,128)(2,1)}, f32[32,2048]{1,0:T(8,128)}, f32[128,512]{1,0:T(8,128)}, f32[49,512]{1,0:T(...) custom-call(bf16[128,512]{1,0:T(8,128)(2,1)} %get-tuple-element.21.refs_0_, bf16[128,512]{1,0:T(8,128)(2,1)} %get-tuple-element.22.refs_1_, ...), custom_call_target="tpu_custom_call" | custom-call | tf_op jit(solution)/shard_map/pallas_call | solution.py:553
